TPU v7x, 512 devices: a whole 4x8x8 slice. The times are simulated.
512 devices in a mesh: section: 16 (over z, x_hi), dp: 32 (over y, x_lo, core).
Axes of the slice: x: 4 (x_hi: 2, x_lo: 2; x = x_hi * 2 + x_lo), y: 8, z: 8, core: 2. Of those that a mesh axis runs over, the one named last changes fastest.
Arguments:
- hidden_in: bfloat16 [8, 512, 8192], P(None, 'dp', 'section'), may hold values from -36 to 36
- cotangent: bfloat16 [8, 512, 8192], P(None, 'dp', 'section'), may hold values from -0.0017089844 to 0.0017089844
- codes_v: int32 [16, 1024, 512], P('section'), may hold values from 0 to 65535, as said below
- zeros_v: int32 [16, 64, 512], P('section'), may hold values from 0 to 3
- steps_v: float32 [16, 64, 512], P('section', None, 'dp'), may hold values from 0.003314563 to 0.014363106
- codes_o: int32 [16, 64, 8192], P('section'), may hold values from 0 to 65535, as said below
- zeros_o: int32 [16, 4, 8192], P('section'), may hold values from 0 to 3
- steps_o: float32 [16, 4, 8192], P('section', None, 'dp'), may hold values from 0.013258252 to 0.057452425
- gain: float32 [16, 8192], P('section'), may hold values from 0.25 to 1.75
Outputs:
- grad_v: float32 [16, 64, 512], P('section', None, 'dp')
- grad_o: float32 [16, 4, 8192], P('section', None, 'dp')
Inputs may be any that keep to these rules, and one draw needn't show every extreme that they name: `codes_v`: word (s, r, c) holds the codes of rows 8 r to 8 r + 7 of column c: the code of row 8 r + j in bits 2 j and 2 j + 1. `codes_o`: word (s, r, c) holds the codes of rows 8 r to 8 r + 7 of column c: the code of row 8 r + j in bits 2 j and 2 j + 1.
All inputs are finite; a program needn't handle non-finite values.
Results may differ from a plain program's by a relative error of at most 0.04.
Values may be sent and summed in bfloat16 or wider, within the bound.
No kernel may reach another device: no remote copies, remote signals or barrier semaphores. Data moves between devices by JAX's collectives and lax.ppermute only.
A program may use at most 128 MiB of HBM per device.

v0:
```python
import jax
import jax.numpy as jnp
from jax import lax
from jax.sharding import PartitionSpec as P

GROUP = 128
PACK = 8


def shifted(value, axis, steps):
    count = lax.axis_size(axis)
    initial, last = (max(0, -steps), min(count, count - steps))
    return lax.ppermute(value, axis, [(source, source + steps) for source in range(initial, last)])


def unpack_codes(packed):
    shifts = 2 * jnp.arange(PACK, dtype=jnp.int32)
    fields = jnp.right_shift(packed[:, None, :], shifts[None, :, None]) & 3
    return fields.reshape(packed.shape[0] * PACK, packed.shape[1])


def centred_codes(packed, zero_points):
    code_table = unpack_codes(packed)
    row_total, col_total = code_table.shape
    grouped = code_table.reshape(row_total // GROUP, GROUP, col_total) - zero_points[:, None, :]
    return grouped.astype(jnp.float32)


def dequantize(packed, zero_points, step_sizes):
    grouped = centred_codes(packed, zero_points)
    return (grouped * step_sizes[:, None, :]).reshape(-1, packed.shape[1]).astype(jnp.bfloat16)


def normalize(states, gain_row):
    widened = states.astype(jnp.float32)
    inverse = lax.rsqrt(jnp.mean(widened * widened, axis=-1, keepdims=True) + 1e-05)
    return (widened, inverse, (widened * inverse * gain_row).astype(jnp.bfloat16))


def forward_layer(states, weight_v, weight_o, gain_row):
    widened, inverse, normed = normalize(states, gain_row)
    values = jnp.dot(normed, weight_v, preferred_element_type=jnp.float32).astype(jnp.bfloat16)
    updated = (widened + jnp.dot(values, weight_o, preferred_element_type=jnp.float32)).astype(
        jnp.bfloat16
    )
    return (updated, values)


def backward_layer(states, upstream, weight_v, weight_o, gain_row):
    widened, inverse, normed = normalize(states, gain_row)
    value_grad = jnp.dot(upstream, weight_o.T, preferred_element_type=jnp.float32).astype(
        jnp.bfloat16
    )
    normed_grad = jnp.dot(value_grad, weight_v.T, preferred_element_type=jnp.float32) * gain_row
    mixed_mean = jnp.mean(normed_grad * widened, axis=-1, keepdims=True)
    state_grad = (
        upstream.astype(jnp.float32)
        + inverse * normed_grad
        - widened * (inverse * inverse * inverse) * mixed_mean
    )
    return (state_grad.astype(jnp.bfloat16), value_grad)


def group_reduce(centred, partial_product):
    row_total, col_total = partial_product.shape
    shaped = partial_product.reshape(row_total // GROUP, GROUP, col_total).astype(jnp.float32)
    return jnp.sum(centred * shaped, axis=1)


def on_device(hidden_in, cotangent, codes_v, zeros_v, steps_v, codes_o, zeros_o, steps_o, gain):
    section_count = lax.axis_size("section")
    section_id = lax.axis_index("section")
    full_v, full_o = (
        lax.all_gather(steps_v, "dp", axis=2, tiled=True),
        lax.all_gather(steps_o, "dp", axis=2, tiled=True),
    )
    first_states, last_grads = (
        lax.all_gather(hidden_in, "section", axis=2, tiled=True),
        lax.all_gather(cotangent, "section", axis=2, tiled=True),
    )
    micro_count, token_count, feature_count = first_states.shape
    packed_v, zero_v, step_v = (codes_v[0], zeros_v[0], full_v[0])
    packed_o, zero_o, step_o = (codes_o[0], zeros_o[0], full_o[0])
    gain_row = gain[0]
    value_width = packed_v.shape[1]

    def weights_now():
        return (dequantize(packed_v, zero_v, step_v), dequantize(packed_o, zero_o, step_o))

    def forward_part(tick_index, loop_state):
        arrived_f, arrived_b, state_store, value_store, grad_store, vgrad_store = loop_state
        micro_index = tick_index - section_id
        active = (micro_index >= 0) & (micro_index < micro_count)
        position = jnp.clip(micro_index, 0, micro_count - 1)
        fresh_rows = lax.dynamic_index_in_dim(first_states, position, 0, keepdims=False)
        states = jnp.where(section_id == 0, fresh_rows, arrived_f)

        def run_layer(stores):
            weight_v, weight_o = weights_now()
            updated, values = forward_layer(states, weight_v, weight_o, gain_row)
            new_states = lax.dynamic_update_index_in_dim(stores[0], states, position, 0)
            new_values = lax.dynamic_update_index_in_dim(stores[1], values, position, 0)
            return (updated, new_states, new_values)

        def skip_layer(stores):
            return (jnp.zeros_like(states), stores[0], stores[1])

        updated, state_store, value_store = lax.cond(
            active, run_layer, skip_layer, (state_store, value_store)
        )
        arrived_f = shifted(updated, "section", 1)
        return (arrived_f, arrived_b, state_store, value_store, grad_store, vgrad_store)

    def backward_part(tick_index, offset, loop_state):
        arrived_f, arrived_b, state_store, value_store, grad_store, vgrad_store = loop_state
        micro_index = tick_index - offset
        active = (micro_index >= 0) & (micro_index < micro_count)
        position = jnp.clip(micro_index, 0, micro_count - 1)
        seed_rows = lax.dynamic_index_in_dim(last_grads, position, 0, keepdims=False)
        upstream = jnp.where(section_id == section_count - 1, seed_rows, arrived_b)

        def run_back(stores):
            weight_v, weight_o = weights_now()
            states = lax.dynamic_index_in_dim(state_store, position, 0, keepdims=False)
            state_grad, value_grad = backward_layer(states, upstream, weight_v, weight_o, gain_row)
            new_grads = lax.dynamic_update_index_in_dim(stores[0], upstream, position, 0)
            new_vgrads = lax.dynamic_update_index_in_dim(stores[1], value_grad, position, 0)
            return (state_grad, new_grads, new_vgrads)

        def skip_back(stores):
            return (jnp.zeros_like(upstream), stores[0], stores[1])

        state_grad, grad_store, vgrad_store = lax.cond(
            active, run_back, skip_back, (grad_store, vgrad_store)
        )
        arrived_b = shifted(state_grad, "section", -1)
        return (arrived_f, arrived_b, state_store, value_store, grad_store, vgrad_store)

    empty_rows = jnp.zeros((token_count, feature_count), jnp.bfloat16)
    loop_state = (
        empty_rows,
        empty_rows,
        jnp.zeros((micro_count, token_count, feature_count), jnp.bfloat16),
        jnp.zeros((micro_count, token_count, value_width), jnp.bfloat16),
        jnp.zeros((micro_count, token_count, feature_count), jnp.bfloat16),
        jnp.zeros((micro_count, token_count, value_width), jnp.bfloat16),
    )
    early_offset = section_count - 1 - section_id

    def back_only(tick_index, current):
        return backward_part(tick_index, early_offset, current)

    loop_state = lax.fori_loop(0, micro_count + section_count - 1, forward_part, loop_state)
    loop_state = lax.fori_loop(0, micro_count + section_count - 1, back_only, loop_state)
    state_store, value_store, grad_store, vgrad_store = (
        loop_state[2],
        loop_state[3],
        loop_state[4],
        loop_state[5],
    )
    row_total = micro_count * token_count
    normed = normalize(state_store.reshape(row_total, feature_count), gain_row)[2]
    part_v = jnp.dot(
        normed.T, vgrad_store.reshape(row_total, value_width), preferred_element_type=jnp.float32
    ).astype(jnp.bfloat16)
    part_o = jnp.dot(
        value_store.reshape(row_total, value_width).T,
        grad_store.reshape(row_total, feature_count),
        preferred_element_type=jnp.float32,
    ).astype(jnp.bfloat16)
    local_v = group_reduce(centred_codes(packed_v, zero_v), part_v)
    local_o = group_reduce(centred_codes(packed_o, zero_o), part_o)
    grad_v, grad_o = (
        lax.psum_scatter(
            local_v[None].astype(jnp.bfloat16), "dp", scatter_dimension=2, tiled=True
        ).astype(jnp.float32),
        lax.psum_scatter(
            local_o[None].astype(jnp.bfloat16), "dp", scatter_dimension=2, tiled=True
        ).astype(jnp.float32),
    )
    return (grad_v, grad_o)


def solution(mesh):
    return jax.shard_map(
        on_device,
        mesh=mesh,
        in_specs=(
            P(None, "dp", "section"),
            P(None, "dp", "section"),
            P("section", None, None),
            P("section", None, None),
            P("section", None, "dp"),
            P("section", None, None),
            P("section", None, None),
            P("section", None, "dp"),
            P("section", None),
        ),
        out_specs=(P("section", None, "dp"), P("section", None, "dp")),
        check_vma=False,
    )
```

profile of v0, /device:TPU:128, one launch (start us, length us, event | category | flops | bytes accessed | tf_op | source)
XLA Modules:
  0.0 1661.2 jit_solution(12213159391350433189)
XLA Ops:
  8.7 35.8 %all_gather.13 = f32[1,64,512]{1,0,2:T(1,128)S(1)} all-gather(f32[1,64,16]{1,0,2:T(1,128)} %bitcast.184), channel_id=1, replica_groups=mesh['section'=16,'dp'=32] {'dp'}, dimensions={2}, use_global_device_ids=true | all-gather | bytes 135168 | tf_op jit(solution)/shard_map/all_gather | solution.py:74
  44.6 31.5 %all_gather.14 = f32[1,4,8192]{2,1,0:T(4,128)S(1)} all-gather(f32[1,4,256]{2,1,0:T(4,128)} %param.24), channel_id=1, replica_groups=mesh['section'=16,'dp'=32] {'dp'}, dimensions={2}, use_global_device_ids=true | all-gather | bytes 135168 | tf_op jit(solution)/shard_map/all_gather | solution.py:75
  76.1 28.4 %all-gather.3.cloned.1.call-done = bf16[8,16,8192]{2,1,0:T(8,128)(2,1)} async-done(((bf16[8,16,512]{2,1,0:T(8,128)(2,1)}), bf16[8,16,8192]{2,1,0:T(8,128)(2,1)}) %all-gather.3.cloned.1.call-update) | async-done | bytes 2097168 | tf_op jit(solution)/shard_map/all_gather | solution.py:78
  106.1 482.1 %while.37 = (s32[]{:T(128)}, bf16[16,8192]{1,0:T(8,128)(2,1)S(1)}, bf16[8,16,8192]{2,1,0:T(8,128)(2,1)}, bf16[8,16,512]{2,1,0:T(8,128)(2,1)S(1)}, s32[]{:T(128)}...) while((s32[]{:T(128)}, bf16[16,8192]{1,0:T(8,128)(2,1)S(1)}, ...), condition=%wide.region_4.5_spmd, body=%wide.region_0.4_spmd.sunk | while | flops 320217120 | bytes 50618608 | solution.py:153
  142.0 62.1 %collective-permute-done = bf16[16,8192]{1,0:T(8,128)(2,1)S(1)} collective-permute-done((bf16[16,8192]{1,0:T(8,128)(2,1)S(1)}, bf16[16,8192]{1,0:T(8,128)(2,1)S(1)}, u32[]{:S(2)}, u32[]{:S(2)}) %collective-permute-start) | collective-permute-done | bytes 262176 | tf_op jit(solution)/shard_map/while/body/eval_jaxpr/ppermute | solution.py:13
  229.1 14.3 conditional.4
  254.1 14.4 conditional.4
  279.1 14.3 conditional.4
  304.1 14.3 conditional.4
  329.1 14.3 conditional.4
  404.1 15.3 collective-permute-start
  434.1 16.3 collective-permute-start
  465.0 17.7 %collective-permute-start = (bf16[16,8192]{1,0:T(8,128)(2,1)S(1)}, bf16[16,8192]{1,0:T(8,128)(2,1)S(1)}, u32[]{:S(2)}, u32[]{:S(2)}) collective-permute-start(bf16[16,8192]{1,0:T(8,128)(2,1)S(1)} %get-tuple-element.1252), channel_id=1, source_target_pairs={{0,32},{32,64},{64,96},{96,128},{128,160},{160,192},{192,224},{224... | collective-permute-start | bytes 786440 | tf_op jit(solution)/shard_map/while/body/eval_jaxpr/ppermute | solution.py:13
  498.5 22.3 %collective-permute-start = (bf16[16,8192]{1,0:T(8,128)(2,1)S(1)}, bf16[16,8192]{1,0:T(8,128)(2,1)S(1)}, u32[]{:S(2)}, u32[]{:S(2)}) collective-permute-start(bf16[16,8192]{1,0:T(8,128)(2,1)S(1)} %get-tuple-element.1252), channel_id=1, source_target_pairs={{0,32},{32,64},{64,96},{96,128},{128,160},{160,192},{192,224},{224... | collective-permute-start | bytes 786440 | tf_op jit(solution)/shard_map/while/body/eval_jaxpr/ppermute | solution.py:13
  591.9 665.1 %while.38 = (s32[]{:T(128)}, bf16[16,8192]{1,0:T(8,128)(2,1)S(1)}, bf16[8,16,8192]{2,1,0:T(8,128)(2,1)}, bf16[8,16,512]{2,1,0:T(8,128)(2,1)S(1)}, s32[]{:T(128)}...) while((s32[]{:T(128)}, bf16[16,8192]{1,0:T(8,128)(2,1)S(1)}, ...), condition=%wide.region_11.12_spmd, body=%wide.region_6.0_spmd.sunk | while | flops 320741440 | bytes 51929288 | solution.py:154
  604.6 15.3 collective-permute-done.1
  636.7 22.6 %collective-permute-done.1 = bf16[16,8192]{1,0:T(8,128)(2,1)S(1)} collective-permute-done((bf16[16,8192]{1,0:T(8,128)(2,1)S(1)}, bf16[16,8192]{1,0:T(8,128)(2,1)S(1)}, u32[]{:S(2)}, u32[]{:S(2)}) %collective-permute-start.1) | collective-permute-done | bytes 262176 | tf_op jit(solution)/shard_map/while/body/eval_jaxpr/ppermute | solution.py:13
  674.3 16.6 collective-permute-done.1
  706.1 20.5 %collective-permute-done.1 = bf16[16,8192]{1,0:T(8,128)(2,1)S(1)} collective-permute-done((bf16[16,8192]{1,0:T(8,128)(2,1)S(1)}, bf16[16,8192]{1,0:T(8,128)(2,1)S(1)}, u32[]{:S(2)}, u32[]{:S(2)}) %collective-permute-start.1) | collective-permute-done | bytes 262176 | tf_op jit(solution)/shard_map/while/body/eval_jaxpr/ppermute | solution.py:13
  751.1 205.7 %collective-permute-done.1 = bf16[16,8192]{1,0:T(8,128)(2,1)S(1)} collective-permute-done((bf16[16,8192]{1,0:T(8,128)(2,1)S(1)}, bf16[16,8192]{1,0:T(8,128)(2,1)S(1)}, u32[]{:S(2)}, u32[]{:S(2)}) %collective-permute-start.1) | collective-permute-done | bytes 262176 | tf_op jit(solution)/shard_map/while/body/eval_jaxpr/ppermute | solution.py:13
  956.9 17.2 %conditional.5 = (bf16[16,8192]{1,0:T(8,128)(2,1)S(1)}, bf16[8,16,8192]{2,1,0:T(8,128)(2,1)}, bf16[8,16,512]{2,1,0:T(8,128)(2,1)S(1)}) conditional(s32[]{:T(128)} %convert_element_type.274, (bf16[8,16,8192]{2,1,0:T(8,128)(2,1)}, bf16[8,16,512]{2,1,0:T(8,128)(2,1)S(1)}) %tuple.121, (pred[]{:T(512)}, s32[]{:T(128)}, bf16[8,16,8192]{2,1,0:T(8,128)(2,1)}, ...), branch_computations={%region_7.7_spmd, %region_8.10_spmd} | conditional | flops 320741440 | bytes 50880340 | solution.py:133
  986.0 17.2 %conditional.5 = (bf16[16,8192]{1,0:T(8,128)(2,1)S(1)}, bf16[8,16,8192]{2,1,0:T(8,128)(2,1)}, bf16[8,16,512]{2,1,0:T(8,128)(2,1)S(1)}) conditional(s32[]{:T(128)} %convert_element_type.274, (bf16[8,16,8192]{2,1,0:T(8,128)(2,1)}, bf16[8,16,512]{2,1,0:T(8,128)(2,1)S(1)}) %tuple.121, (pred[]{:T(512)}, s32[]{:T(128)}, bf16[8,16,8192]{2,1,0:T(8,128)(2,1)}, ...), branch_computations={%region_7.7_spmd, %region_8.10_spmd} | conditional | flops 320741440 | bytes 50880340 | solution.py:133
  1015.1 17.2 %conditional.5 = (bf16[16,8192]{1,0:T(8,128)(2,1)S(1)}, bf16[8,16,8192]{2,1,0:T(8,128)(2,1)}, bf16[8,16,512]{2,1,0:T(8,128)(2,1)S(1)}) conditional(s32[]{:T(128)} %convert_element_type.274, (bf16[8,16,8192]{2,1,0:T(8,128)(2,1)}, bf16[8,16,512]{2,1,0:T(8,128)(2,1)S(1)}) %tuple.121, (pred[]{:T(512)}, s32[]{:T(128)}, bf16[8,16,8192]{2,1,0:T(8,128)(2,1)}, ...), branch_computations={%region_7.7_spmd, %region_8.10_spmd} | conditional | flops 320741440 | bytes 50880340 | solution.py:133
  1044.3 17.3 %conditional.5 = (bf16[16,8192]{1,0:T(8,128)(2,1)S(1)}, bf16[8,16,8192]{2,1,0:T(8,128)(2,1)}, bf16[8,16,512]{2,1,0:T(8,128)(2,1)S(1)}) conditional(s32[]{:T(128)} %convert_element_type.274, (bf16[8,16,8192]{2,1,0:T(8,128)(2,1)}, bf16[8,16,512]{2,1,0:T(8,128)(2,1)S(1)}) %tuple.121, (pred[]{:T(512)}, s32[]{:T(128)}, bf16[8,16,8192]{2,1,0:T(8,128)(2,1)}, ...), branch_computations={%region_7.7_spmd, %region_8.10_spmd} | conditional | flops 320741440 | bytes 50880340 | solution.py:133
  1073.4 17.2 %conditional.5 = (bf16[16,8192]{1,0:T(8,128)(2,1)S(1)}, bf16[8,16,8192]{2,1,0:T(8,128)(2,1)}, bf16[8,16,512]{2,1,0:T(8,128)(2,1)S(1)}) conditional(s32[]{:T(128)} %convert_element_type.274, (bf16[8,16,8192]{2,1,0:T(8,128)(2,1)}, bf16[8,16,512]{2,1,0:T(8,128)(2,1)S(1)}) %tuple.121, (pred[]{:T(512)}, s32[]{:T(128)}, bf16[8,16,8192]{2,1,0:T(8,128)(2,1)}, ...), branch_computations={%region_7.7_spmd, %region_8.10_spmd} | conditional | flops 320741440 | bytes 50880340 | solution.py:133
  1102.4 17.2 %conditional.5 = (bf16[16,8192]{1,0:T(8,128)(2,1)S(1)}, bf16[8,16,8192]{2,1,0:T(8,128)(2,1)}, bf16[8,16,512]{2,1,0:T(8,128)(2,1)S(1)}) conditional(s32[]{:T(128)} %convert_element_type.274, (bf16[8,16,8192]{2,1,0:T(8,128)(2,1)}, bf16[8,16,512]{2,1,0:T(8,128)(2,1)S(1)}) %tuple.121, (pred[]{:T(512)}, s32[]{:T(128)}, bf16[8,16,8192]{2,1,0:T(8,128)(2,1)}, ...), branch_computations={%region_7.7_spmd, %region_8.10_spmd} | conditional | flops 320741440 | bytes 50880340 | solution.py:133
  1131.6 17.2 %conditional.5 = (bf16[16,8192]{1,0:T(8,128)(2,1)S(1)}, bf16[8,16,8192]{2,1,0:T(8,128)(2,1)}, bf16[8,16,512]{2,1,0:T(8,128)(2,1)S(1)}) conditional(s32[]{:T(128)} %convert_element_type.274, (bf16[8,16,8192]{2,1,0:T(8,128)(2,1)}, bf16[8,16,512]{2,1,0:T(8,128)(2,1)S(1)}) %tuple.121, (pred[]{:T(512)}, s32[]{:T(128)}, bf16[8,16,8192]{2,1,0:T(8,128)(2,1)}, ...), branch_computations={%region_7.7_spmd, %region_8.10_spmd} | conditional | flops 320741440 | bytes 50880340 | solution.py:133
  1162.5 17.2 %conditional.5 = (bf16[16,8192]{1,0:T(8,128)(2,1)S(1)}, bf16[8,16,8192]{2,1,0:T(8,128)(2,1)}, bf16[8,16,512]{2,1,0:T(8,128)(2,1)S(1)}) conditional(s32[]{:T(128)} %convert_element_type.274, (bf16[8,16,8192]{2,1,0:T(8,128)(2,1)}, bf16[8,16,512]{2,1,0:T(8,128)(2,1)S(1)}) %tuple.121, (pred[]{:T(512)}, s32[]{:T(128)}, bf16[8,16,8192]{2,1,0:T(8,128)(2,1)}, ...), branch_computations={%region_7.7_spmd, %region_8.10_spmd} | conditional | flops 320741440 | bytes 50880340 | solution.py:133
  1189.5 20.0 %collective-permute-start.1 = (bf16[16,8192]{1,0:T(8,128)(2,1)S(1)}, bf16[16,8192]{1,0:T(8,128)(2,1)S(1)}, u32[]{:S(2)}, u32[]{:S(2)}) collective-permute-start(bf16[16,8192]{1,0:T(8,128)(2,1)S(1)} %get-tuple-element.1270), channel_id=1, source_target_pairs={{32,0},{64,32},{96,64},{128,96},{160,128},{192,160},{224,192},{256... | collective-permute-start | bytes 786440 | tf_op jit(solution)/shard_map/while/body/eval_jaxpr/ppermute | solution.py:13
  1224.2 18.2 %collective-permute-start.1 = (bf16[16,8192]{1,0:T(8,128)(2,1)S(1)}, bf16[16,8192]{1,0:T(8,128)(2,1)S(1)}, u32[]{:S(2)}, u32[]{:S(2)}) collective-permute-start(bf16[16,8192]{1,0:T(8,128)(2,1)S(1)} %get-tuple-element.1270), channel_id=1, source_target_pairs={{32,0},{64,32},{96,64},{128,96},{160,128},{192,160},{224,192},{256... | collective-permute-start | bytes 786440 | tf_op jit(solution)/shard_map/while/body/eval_jaxpr/ppermute | solution.py:13
  1294.4 233.6 %all-reduce.3.cloned.1.call-done = bf16[1,64,512]{1,0,2:T(2,128)(2,1)} async-done(((bf16[1,64,512]{1,0,2:T(2,128)(2,1)}), bf16[1,64,512]{1,0,2:T(2,128)(2,1)}) %all-reduce.3.cloned.1.call-update) | async-done | bytes 65552
  1529.4 123.7 %reduce-scatter.4.cloned.1.call-done = bf16[256,4]{1,0:T(8,128)(2,1)} async-done(((bf16[8192,4]{1,0:T(8,128)(2,1)}), bf16[256,4]{1,0:T(8,128)(2,1)}) %reduce-scatter.4.cloned.1.call-update) | async-done | bytes 2064
  (468 shorter events, 782.5 us)
Async XLA Ops:
  7.2 97.3 %all-gather.3.cloned.1.call-start = ((), (), s32[]{:S(2)}) async-start(), calls=%async_computation.1 | async-start | bytes 2228224 | tf_op jit(solution)/shard_map/all_gather | solution.py:78
  7.9 582.4 %all-gather.5.cloned.1.call-start = ((), (), s32[]{:S(2)}) async-start(), calls=%async_computation.2 | async-start | bytes 2228224 | tf_op jit(solution)/shard_map/all_gather | solution.py:79
  8.6 1519.4 %all-reduce.3.cloned.1.call-start = ((), (), s32[]{:S(2)}) async-start(), calls=%async_computation.4 | async-start | bytes 524288
  139.2 64.8 %collective-permute-start = (bf16[16,8192]{1,0:T(8,128)(2,1)S(1)}, bf16[16,8192]{1,0:T(8,128)(2,1)S(1)}, u32[]{:S(2)}, u32[]{:S(2)}) collective-permute-start(bf16[16,8192]{1,0:T(8,128)(2,1)S(1)} %get-tuple-element.1252), channel_id=1, source_target_pairs={{0,32},{32,64},{64,96},{96,128},{128,160},{160,192},{192,224},{224... | collective-permute-start | bytes 786440 | tf_op jit(solution)/shard_map/while/body/eval_jaxpr/ppermute | solution.py:13
  404.1 19.2 %collective-permute-start = (bf16[16,8192]{1,0:T(8,128)(2,1)S(1)}, bf16[16,8192]{1,0:T(8,128)(2,1)S(1)}, u32[]{:S(2)}, u32[]{:S(2)}) collective-permute-start(bf16[16,8192]{1,0:T(8,128)(2,1)S(1)} %get-tuple-element.1252), channel_id=1, source_target_pairs={{0,32},{32,64},{64,96},{96,128},{128,160},{160,192},{192,224},{224... | collective-permute-start | bytes 786440 | tf_op jit(solution)/shard_map/while/body/eval_jaxpr/ppermute | solution.py:13
  434.1 20.1 %collective-permute-start = (bf16[16,8192]{1,0:T(8,128)(2,1)S(1)}, bf16[16,8192]{1,0:T(8,128)(2,1)S(1)}, u32[]{:S(2)}, u32[]{:S(2)}) collective-permute-start(bf16[16,8192]{1,0:T(8,128)(2,1)S(1)} %get-tuple-element.1252), channel_id=1, source_target_pairs={{0,32},{32,64},{64,96},{96,128},{128,160},{160,192},{192,224},{224... | collective-permute-start | bytes 786440 | tf_op jit(solution)/shard_map/while/body/eval_jaxpr/ppermute | solution.py:13
  465.0 21.5 %collective-permute-start = (bf16[16,8192]{1,0:T(8,128)(2,1)S(1)}, bf16[16,8192]{1,0:T(8,128)(2,1)S(1)}, u32[]{:S(2)}, u32[]{:S(2)}) collective-permute-start(bf16[16,8192]{1,0:T(8,128)(2,1)S(1)} %get-tuple-element.1252), channel_id=1, source_target_pairs={{0,32},{32,64},{64,96},{96,128},{128,160},{160,192},{192,224},{224... | collective-permute-start | bytes 786440 | tf_op jit(solution)/shard_map/while/body/eval_jaxpr/ppermute | solution.py:13
  486.5 11.9 collective-permute-start
  498.5 26.2 %collective-permute-start = (bf16[16,8192]{1,0:T(8,128)(2,1)S(1)}, bf16[16,8192]{1,0:T(8,128)(2,1)S(1)}, u32[]{:S(2)}, u32[]{:S(2)}) collective-permute-start(bf16[16,8192]{1,0:T(8,128)(2,1)S(1)} %get-tuple-element.1252), channel_id=1, source_target_pairs={{0,32},{32,64},{64,96},{96,128},{128,160},{160,192},{192,224},{224... | collective-permute-start | bytes 786440 | tf_op jit(solution)/shard_map/while/body/eval_jaxpr/ppermute | solution.py:13
  524.7 15.0 collective-permute-start
  539.7 14.8 collective-permute-start
  554.6 17.3 %collective-permute-start = (bf16[16,8192]{1,0:T(8,128)(2,1)S(1)}, bf16[16,8192]{1,0:T(8,128)(2,1)S(1)}, u32[]{:S(2)}, u32[]{:S(2)}) collective-permute-start(bf16[16,8192]{1,0:T(8,128)(2,1)S(1)} %get-tuple-element.1252), channel_id=1, source_target_pairs={{0,32},{32,64},{64,96},{96,128},{128,160},{160,192},{192,224},{224... | collective-permute-start | bytes 786440 | tf_op jit(solution)/shard_map/while/body/eval_jaxpr/ppermute | solution.py:13
  571.9 16.3 collective-permute-start
  602.2 17.7 %collective-permute-start.1 = (bf16[16,8192]{1,0:T(8,128)(2,1)S(1)}, bf16[16,8192]{1,0:T(8,128)(2,1)S(1)}, u32[]{:S(2)}, u32[]{:S(2)}) collective-permute-start(bf16[16,8192]{1,0:T(8,128)(2,1)S(1)} %get-tuple-element.1270), channel_id=1, source_target_pairs={{32,0},{64,32},{96,64},{128,96},{160,128},{192,160},{224,192},{256... | collective-permute-start | bytes 786440 | tf_op jit(solution)/shard_map/while/body/eval_jaxpr/ppermute | solution.py:13
  620.0 14.8 collective-permute-start.1
  634.8 24.5 %collective-permute-start.1 = (bf16[16,8192]{1,0:T(8,128)(2,1)S(1)}, bf16[16,8192]{1,0:T(8,128)(2,1)S(1)}, u32[]{:S(2)}, u32[]{:S(2)}) collective-permute-start(bf16[16,8192]{1,0:T(8,128)(2,1)S(1)} %get-tuple-element.1270), channel_id=1, source_target_pairs={{32,0},{64,32},{96,64},{128,96},{160,128},{192,160},{224,192},{256... | collective-permute-start | bytes 786440 | tf_op jit(solution)/shard_map/while/body/eval_jaxpr/ppermute | solution.py:13
  659.4 13.0 collective-permute-start.1
  672.4 18.5 %collective-permute-start.1 = (bf16[16,8192]{1,0:T(8,128)(2,1)S(1)}, bf16[16,8192]{1,0:T(8,128)(2,1)S(1)}, u32[]{:S(2)}, u32[]{:S(2)}) collective-permute-start(bf16[16,8192]{1,0:T(8,128)(2,1)S(1)} %get-tuple-element.1270), channel_id=1, source_target_pairs={{32,0},{64,32},{96,64},{128,96},{160,128},{192,160},{224,192},{256... | collective-permute-start | bytes 786440 | tf_op jit(solution)/shard_map/while/body/eval_jaxpr/ppermute | solution.py:13
  690.9 13.2 collective-permute-start.1
  704.1 22.4 %collective-permute-start.1 = (bf16[16,8192]{1,0:T(8,128)(2,1)S(1)}, bf16[16,8192]{1,0:T(8,128)(2,1)S(1)}, u32[]{:S(2)}, u32[]{:S(2)}) collective-permute-start(bf16[16,8192]{1,0:T(8,128)(2,1)S(1)} %get-tuple-element.1270), channel_id=1, source_target_pairs={{32,0},{64,32},{96,64},{128,96},{160,128},{192,160},{224,192},{256... | collective-permute-start | bytes 786440 | tf_op jit(solution)/shard_map/while/body/eval_jaxpr/ppermute | solution.py:13
  736.4 11.7 collective-permute-start.1
  748.2 208.7 %collective-permute-start.1 = (bf16[16,8192]{1,0:T(8,128)(2,1)S(1)}, bf16[16,8192]{1,0:T(8,128)(2,1)S(1)}, u32[]{:S(2)}, u32[]{:S(2)}) collective-permute-start(bf16[16,8192]{1,0:T(8,128)(2,1)S(1)} %get-tuple-element.1270), channel_id=1, source_target_pairs={{32,0},{64,32},{96,64},{128,96},{160,128},{192,160},{224,192},{256... | collective-permute-start | bytes 786440 | tf_op jit(solution)/shard_map/while/body/eval_jaxpr/ppermute | solution.py:13
  974.1 11.9 collective-permute-start.1
  1003.3 11.8 collective-permute-start.1
  1032.3 12.0 collective-permute-start.1
  1061.5 11.8 collective-permute-start.1
  1090.6 11.9 collective-permute-start.1
  1119.7 11.9 collective-permute-start.1
  1148.8 13.7 collective-permute-start.1
  1189.5 23.9 %collective-permute-start.1 = (bf16[16,8192]{1,0:T(8,128)(2,1)S(1)}, bf16[16,8192]{1,0:T(8,128)(2,1)S(1)}, u32[]{:S(2)}, u32[]{:S(2)}) collective-permute-start(bf16[16,8192]{1,0:T(8,128)(2,1)S(1)} %get-tuple-element.1270), channel_id=1, source_target_pairs={{32,0},{64,32},{96,64},{128,96},{160,128},{192,160},{224,192},{256... | collective-permute-start | bytes 786440 | tf_op jit(solution)/shard_map/while/body/eval_jaxpr/ppermute | solution.py:13
  1224.2 22.1 %collective-permute-start.1 = (bf16[16,8192]{1,0:T(8,128)(2,1)S(1)}, bf16[16,8192]{1,0:T(8,128)(2,1)S(1)}, u32[]{:S(2)}, u32[]{:S(2)}) collective-permute-start(bf16[16,8192]{1,0:T(8,128)(2,1)S(1)} %get-tuple-element.1270), channel_id=1, source_target_pairs={{32,0},{64,32},{96,64},{128,96},{160,128},{192,160},{224,192},{256... | collective-permute-start | bytes 786440 | tf_op jit(solution)/shard_map/while/body/eval_jaxpr/ppermute | solution.py:13
  1270.8 382.3 %reduce-scatter.4.cloned.1.call-start = ((), (), s32[]{:S(2)}) async-start(), calls=%async_computation.3 | async-start | bytes 2162688
  (68 other events, 570.7 us)
Sparse Core Ops, SparseCore 0:
  11.1 93.4 all-gather.2
  107.6 97.8 all-gather.4
  1270.9 257.1 all-reduce.2
  1530.9 122.0 reduce-scatter.3
where the time goes:
time: 1670 us; the launch traced here: 1660 us
  waiting for transfers between devices  1030 us (62%)
  starting transfers between devices  253 us (15%)
  other arithmetic  189 us (11%)
  matrix products  86.6 us (5%)
  blocking collectives  67.3 us (4%)
  local copies, waits for them, and re-layouts  20.9 us (1%)
    ppermute x46, waiting for transfers between devices, shifted(): lax.ppermute(value, axis, [(source, source + steps) for source in range(i...  639 us
    unnamed x6, waiting for transfers between devices  359 us
    ppermute x46, starting transfers between devices, shifted(): lax.ppermute(value, axis, [(source, source + steps) for source in range(i...  253 us
    convert_element_type x32, other arithmetic, dequantize(): (grouped * step_sizes[:, None, :]).reshape(-1, packed.shape[1])  146 us
    all_gather x1, blocking collectives, on_device(): lax.all_gather(steps_v, 'dp', axis=2, tiled=True)  35.8 us
  transfers between devices with their start and end apart: 50, of which 49 were waited for; matrix products, arithmetic and copies ran while one was open for 9% of the time, Pallas kernels for 0%

commit v1 on v0

v1 whole, which is shorter than its diff:
```python
import jax
import jax.numpy as jnp
from jax import lax
from jax.experimental import pallas as pl
from jax.experimental.pallas import tpu as pltpu
from jax.sharding import PartitionSpec as P

F32, BF16, I32, F8 = jnp.float32, jnp.bfloat16, jnp.int32, jnp.float8_e4m3fn
GROUP = 128
LANES = 128
VMEM_BYTES = 24 * 2**20
STEP_V_MAX = 0.0144
STEP_O_MAX = 0.0575
F8_TOP = 400.0


def pair_words(words):
    rows, cols = words.shape
    shaped = words.reshape(rows // 16, 2, 8, cols)
    return (shaped[:, 0] | (shaped[:, 1] << 16)).reshape(rows // 2, cols)


def order_matrices():
    place = jnp.arange(LANES, dtype=I32)
    field, row = place // 8, place % 8
    natural = jnp.where(field < 8, 8 * row + field, 64 + 8 * row + field - 8)
    gather = (jnp.arange(LANES, dtype=I32)[:, None] == natural[None, :]).astype(BF16)
    return gather, gather.T


def centred_planes(words, zeros):
    planes = []
    for field in range(16):
        part = lax.shift_right_logical(words, jnp.int32(2 * field))
        if field < 15:
            part = part & 3
        planes.append(part.astype(F32) - zeros)
    return jnp.concatenate(planes, axis=0)


def unpack_kernel(own_v_ref, far_v_ref, own_o_ref, far_o_ref, qv_ref, qo_ref):
    groups_v, groups_o = qv_ref.shape[1] // GROUP, qo_ref.shape[1] // GROUP
    for place, (v_ref, o_ref) in enumerate(((own_v_ref, own_o_ref), (far_v_ref, far_o_ref))):

        def v_group(group, carry):
            words = v_ref[pl.ds(pl.multiple_of(group * 8, 8), 8), :]
            zeros = v_ref[pl.ds(groups_v * 8 + group, 1), :].astype(F32)
            at = pl.ds(pl.multiple_of(group * GROUP, GROUP), GROUP)
            qv_ref[place, at, :] = centred_planes(words, zeros).astype(BF16).astype(F8)
            return carry

        lax.fori_loop(0, groups_v, v_group, 0, unroll=4)

        def o_cols(block, carry):
            cols = pl.ds(pl.multiple_of(block * 512, 512), 512)
            for group in range(groups_o):
                words = o_ref[group * 8:group * 8 + 8, cols]
                zeros = o_ref[groups_o * 8 + group:groups_o * 8 + group + 1, cols].astype(F32)
                at = slice(group * GROUP, (group + 1) * GROUP)
                qo_ref[place, at, cols] = centred_planes(words, zeros).astype(BF16).astype(F8)
            return carry

        lax.fori_loop(0, qo_ref.shape[2] // 512, o_cols, 0)


def split8(value):
    high = value.astype(F8).astype(F32)
    return high, (value - high) * 16.0


def merge8(out, start):
    return out[start:start + 16] + out[start + 16:start + 32] * 0.0625


def diag_pair(first, second):
    zero = jnp.zeros_like(first)
    return jnp.concatenate(
        [jnp.concatenate([first, zero], axis=1), jnp.concatenate([zero, second], axis=1)], axis=0
    )


def blocks_down(value):
    return jnp.concatenate([value[:, at:at + LANES] for at in range(0, value.shape[1], LANES)], axis=0)


def blocks_across(value, rows):
    return jnp.concatenate([value[at:at + rows] for at in range(0, value.shape[0], rows)], axis=1)


def row_inverse(states):
    return lax.rsqrt(jnp.mean(states * states, axis=-1, keepdims=True) + 1e-05)


def forward_layer(states, qv, qo, sv, so, gain_row, order, uv_ref, uo_ref):
    rows, width = states.shape
    normed = (states * row_inverse(states) * gain_row).astype(BF16)
    high, low = split8(jnp.dot(blocks_down(normed), order, preferred_element_type=F32))
    groups = width // GROUP
    tiles = jnp.concatenate(
        [high.reshape(groups, rows, LANES), low.reshape(groups, rows, LANES)], axis=1
    ).astype(F8)
    total = jnp.zeros((rows, sv.shape[1]), F32)
    for group in range(0, groups, 2):
        out = jnp.dot(
            diag_pair(tiles[group], tiles[group + 1]),
            qv[group * GROUP:(group + 2) * GROUP, :],
            preferred_element_type=F32,
        )
        for place in range(2):
            unit = merge8(out, 32 * place)
            uv_ref[group + place] = unit.astype(BF16)
            total = total + unit * sv[group + place:group + place + 1, :]
    values = total.astype(BF16)
    ordered = jnp.dot(blocks_down(values), order, preferred_element_type=F32)
    peak = jnp.maximum(jnp.max(jnp.abs(values.astype(F32)), axis=-1, keepdims=True), 1e-37)
    groups_o = values.shape[1] // GROUP
    tiles_o = []
    for group in range(groups_o):
        high, low = split8(ordered[group * rows:(group + 1) * rows] * (1.0 / peak) * F8_TOP)
        tiles_o.append(jnp.concatenate([high, low], axis=0).astype(F8))
    pairs = [diag_pair(tiles_o[group], tiles_o[group + 1]) for group in range(0, groups_o, 2)]
    back = peak * (1.0 / F8_TOP)
    updated = []
    for at in range(0, width, 512):
        moved = states[:, at:at + 512]
        for index, pair in enumerate(pairs):
            out = jnp.dot(pair, qo[index * 256:(index + 1) * 256, at:at + 512], preferred_element_type=F32)
            for place in range(2):
                group = 2 * index + place
                unit = merge8(out, 32 * place) * back
                uo_ref[group, :, at:at + 512] = unit.astype(BF16)
                moved = moved + unit * so[group:group + 1, at:at + 512]
        updated.append(moved.astype(BF16))
    return jnp.concatenate(updated, axis=1)


def forward_kernel(aliased, flag_ref, arrived_ref, fresh_ref, qv_ref, qo_ref, sv_ref, so_ref, gain_ref, order_ref, *rest):
    if aliased:
        rest = rest[3:]
    out_ref, states_hbm, uv_hbm, uo_hbm, states_ref, uv_ref, uo_ref, sems = rest
    first, swap, slot = flag_ref[0], flag_ref[1], flag_ref[2]
    out_ref[...] = jnp.where(first == 1, fresh_ref[...], arrived_ref[...])
    order = order_ref[...]

    def copies(index):
        return [
            pltpu.make_async_copy(here.at[index], there.at[slot, index], sems.at[index, at])
            for at, (here, there) in enumerate(((states_ref, states_hbm), (uv_ref, uv_hbm), (uo_ref, uo_hbm)))
        ]

    def layer(index, carry):
        place = index ^ swap
        states = out_ref[...]
        states_ref[index] = states
        out_ref[...] = forward_layer(
            states.astype(F32), qv_ref.at[place], qo_ref.at[place], sv_ref.at[place], so_ref.at[place],
            gain_ref[place], order, uv_ref.at[index], uo_ref.at[index])
        for copy in copies(index):
            copy.start()
        return carry

    lax.fori_loop(0, 2, layer, 0)
    for index in range(2):
        for copy in copies(index):
            copy.wait()


def backward_layer(upstream, states, qv, qo, sv, so, gain_row, unorder):
    rows, width = upstream.shape
    peak = jnp.maximum(jnp.max(jnp.abs(upstream), axis=-1, keepdims=True), 1e-37)
    scaled = upstream * (1.0 / peak) * (F8_TOP / STEP_O_MAX)
    groups_o = so.shape[0]
    found = []
    for group in range(0, groups_o, 2):
        parts = []
        for place in range(2):
            high, low = split8(scaled * so[group + place:group + place + 1, :])
            parts += [high, low]
        left = jnp.concatenate(parts, axis=0).astype(F8)
        out = lax.dot_general(left, qo[group * GROUP:(group + 2) * GROUP, :], (((1,), (1,)), ((), ())),
                              preferred_element_type=F32)
        found += [merge8(out[:, :LANES], 0), merge8(out[:, LANES:], 32)]
    vgrad = jnp.concatenate(found, axis=0).reshape(groups_o, rows, LANES) * (peak * (STEP_O_MAX / F8_TOP))
    vgrad = vgrad.reshape(groups_o * rows, LANES).astype(BF16)
    vgrad = blocks_across(jnp.dot(vgrad, unorder, preferred_element_type=F32), rows)
    peak = jnp.maximum(jnp.max(jnp.abs(vgrad), axis=-1, keepdims=True), 1e-37)
    scaled = vgrad * (1.0 / peak) * (F8_TOP / STEP_V_MAX)
    found = []
    for group in range(0, width // GROUP, 2):
        parts = []
        for place in range(2):
            high, low = split8(scaled * sv[group + place:group + place + 1, :])
            parts += [high, low]
        left = jnp.concatenate(parts, axis=0).astype(F8)
        out = lax.dot_general(left, qv[group * GROUP:(group + 2) * GROUP, :], (((1,), (1,)), ((), ())),
                              preferred_element_type=F32)
        found += [merge8(out[:, :LANES], 0).astype(BF16), merge8(out[:, LANES:], 32).astype(BF16)]
    ngrad = jnp.dot(jnp.concatenate(found, axis=0), unorder, preferred_element_type=F32)
    ngrad = blocks_across(ngrad, rows) * gain_row * (peak * (STEP_V_MAX / F8_TOP))
    inverse = row_inverse(states)
    mixed = jnp.mean(ngrad * states, axis=-1, keepdims=True)
    moved = upstream + inverse * ngrad - states * (inverse * inverse * inverse) * mixed
    return moved.astype(BF16), vgrad.astype(BF16)


def backward_kernel(flag_ref, arrived_ref, fresh_ref, states_hbm, qv_ref, qo_ref, sv_ref, so_ref, gain_ref,
                    unorder_ref, out_ref, upstream_ref, vgrad_ref, states_ref, sem):
    last, swap, slot = flag_ref[0], flag_ref[1], flag_ref[2]
    copy = pltpu.make_async_copy(states_hbm.at[slot], states_ref, sem)
    copy.start()
    out_ref[...] = jnp.where(last == 1, fresh_ref[...], arrived_ref[...])
    unorder = unorder_ref[...]
    copy.wait()

    def layer(step, carry):
        index = 1 - step
        place = index ^ swap
        upstream = out_ref[...]
        upstream_ref[index] = upstream
        moved, vgrad = backward_layer(
            upstream.astype(F32), states_ref[index].astype(F32), qv_ref.at[place], qo_ref.at[place],
            sv_ref.at[place], so_ref.at[place], gain_ref[place], unorder)
        out_ref[...] = moved
        vgrad_ref[index] = vgrad
        return carry

    lax.fori_loop(0, 2, layer, 0)


def grads_kernel(flag_ref, upstream_ref, vgrad_ref, uv_hbm, uo_hbm, gv_in, go_in, gv_ref, go_ref, uv_ref, uo_ref, sems):
    slot, active = flag_ref[2], flag_ref[3] == 1

    def copies(index):
        return [
            pltpu.make_async_copy(there.at[slot, index], here.at[index], sems.at[index, at])
            for at, (here, there) in enumerate(((uv_ref, uv_hbm), (uo_ref, uo_hbm)))
        ]

    for index in range(2):
        for copy in copies(index):
            copy.start()

    def layer(index, carry):
        for copy in copies(index):
            copy.wait()
        vgrad = vgrad_ref[index].astype(F32)
        for block in range(0, uv_ref.shape[1], 8):
            sums = [jnp.sum(uv_ref[index, block + at].astype(F32) * vgrad, axis=0, keepdims=True) for at in range(8)]
            added = jnp.concatenate(sums, axis=0)
            old = gv_in[index, block:block + 8, :]
            gv_ref[index, block:block + 8, :] = jnp.where(active, old + added, old)
        for group in range(uo_ref.shape[1]):
            for at in range(0, upstream_ref.shape[2], 1024):
                up = upstream_ref[index, :, at:at + 1024].astype(F32)
                added = jnp.sum(uo_ref[index, group, :, at:at + 1024].astype(F32) * up, axis=0, keepdims=True)
                old = go_in[index, group:group + 1, at:at + 1024]
                go_ref[index, group:group + 1, at:at + 1024] = jnp.where(active, old + added, old)
        return carry

    lax.fori_loop(0, 2, layer, 0)


VMEM = pl.BlockSpec(memory_space=pltpu.VMEM)
SMEM = pl.BlockSpec(memory_space=pltpu.SMEM)
ANY = pl.BlockSpec(memory_space=pl.ANY)


def kernel_call(body, outs, in_specs, out_specs, scratch=(), aliases=None, flops=0, moved=0, name=None):
    return pl.pallas_call(
        body,
        out_shape=outs,
        in_specs=in_specs,
        out_specs=out_specs,
        scratch_shapes=list(scratch),
        input_output_aliases=aliases or {},
        compiler_params=pltpu.CompilerParams(vmem_limit_bytes=VMEM_BYTES),
        cost_estimate=pl.CostEstimate(flops=flops, bytes_accessed=moved, transcendentals=0),
        name=name,
    )


def fixed_swap(value, axis, bit):
    count = lax.axis_size(axis)
    return lax.ppermute(value, axis, [(source, source ^ bit) for source in range(count)])


def in_order(bit, mine, other, axis):
    low = jnp.where(bit == 0, mine, other)
    high = jnp.where(bit == 0, other, mine)
    return jnp.concatenate([low, high], axis=axis)


def ends_rows(hidden_in, cotangent, section_id):
    z, side = section_id // 2, section_id % 2
    count = lax.axis_size("section")
    half = hidden_in.shape[0] // 2
    both = jnp.stack([hidden_in, cotangent])
    keep = jnp.where(side == 0, both[:, :half], both[:, half:])
    send = jnp.where(side == 0, both[:, half:], both[:, :half])
    pair = in_order(side, keep, fixed_swap(send, "section", 1), 3)
    even = z % 2 == 0
    held = jnp.where(even, pair[0], pair[1])
    sent = jnp.where(even, pair[1], pair[0])
    held = in_order(z % 2, held, fixed_swap(sent, "section", 2), 2)
    span = 2
    while 2 * span < count:
        routes = []
        for place in range(0, count // 2, 2 * span):
            for side_at in range(2):
                routes.append((2 * (place + span) + side_at, 2 * place + side_at))
                routes.append((2 * (place + span - 1) + side_at, 2 * (place + 2 * span - 1) + side_at))
        held = in_order(z % 2, held, lax.ppermute(held, "section", routes), 2)
        span *= 2
    return held


def gather_steps(value):
    dp_id = lax.axis_index("dp")
    value = value[None]
    bit = 1
    while bit < lax.axis_size("dp"):
        value = in_order((dp_id // bit) % 2, value, fixed_swap(value, "dp", bit), 0)
        bit *= 2
    return value


def scatter_sums(value, side):
    mine = jnp.where(side == 0, value[0], value[1])
    other = jnp.where(side == 0, value[1], value[0])
    total = mine + fixed_swap(other.astype(BF16), "section", 1).astype(F32)
    dp_id = lax.axis_index("dp")
    bit = 1
    while bit < lax.axis_size("dp"):
        split = total.reshape(-1, 2, total.shape[-1])
        place = (dp_id // bit) % 2
        keep = jnp.where(place == 0, split[:, 0], split[:, 1])
        send = jnp.where(place == 0, split[:, 1], split[:, 0])
        total = keep + fixed_swap(send.astype(BF16), "dp", bit).astype(F32)
        bit *= 2
    return total.reshape(-1)


def on_device(hidden_in, cotangent, codes_v, zeros_v, steps_v, codes_o, zeros_o, steps_o, gain):
    section_id = lax.axis_index("section")
    section_count = lax.axis_size("section")
    dp_count = lax.axis_size("dp")
    z, side = section_id // 2, section_id % 2
    stages = section_count // 2
    micro = hidden_in.shape[0] // 2
    rows = hidden_in.shape[1]
    width, value_width = gain.shape[1], codes_v.shape[2]
    groups_v, groups_o = zeros_v.shape[1], zeros_o.shape[1]

    ends = ends_rows(hidden_in, cotangent, section_id)
    own_v = jnp.concatenate([pair_words(codes_v[0]), zeros_v[0]], axis=0)
    own_o = jnp.concatenate([pair_words(codes_o[0]), zeros_o[0]], axis=0)
    far_v, far_o = fixed_swap(own_v, "section", 1), fixed_swap(own_o, "section", 1)
    own_f = jnp.concatenate([steps_v.reshape(-1), steps_o.reshape(-1), gain.reshape(-1)])
    far_f = fixed_swap(own_f, "section", 1)
    both_f = jnp.stack([own_f, far_f])
    count_v, count_o = steps_v.size, steps_o.size
    gains = both_f[:, None, count_v + count_o:]
    steps = gather_steps(both_f[:, :count_v + count_o])
    sv = steps[:, :, :count_v].reshape(dp_count, 2, groups_v, -1).transpose(1, 2, 0, 3).reshape(2, groups_v, value_width)
    so = steps[:, :, count_v:].reshape(dp_count, 2, groups_o, -1).transpose(1, 2, 0, 3).reshape(2, groups_o, width)
    order, unorder = order_matrices()

    qv, qo = kernel_call(
        unpack_kernel,
        (jax.ShapeDtypeStruct((2, width, value_width), F8), jax.ShapeDtypeStruct((2, value_width, width), F8)),
        [VMEM] * 4, (VMEM, VMEM), flops=10**8, moved=2**22, name="unpack",
    )(own_v, far_v, own_o, far_o)

    uv_shape, uo_shape = (2, groups_v, rows, value_width), (2, groups_o, rows, width)
    stored = [(2, rows, width), uv_shape, uo_shape]
    slots = None
    flops = 4 * 2 * rows * width * value_width * 2

    def forward(tick, arrived, slots):
        position = tick - z
        active = (position >= 0) & (position < micro)
        slot = jnp.where(active, position, micro)
        flag = jnp.stack([z == 0, side, slot]).astype(I32)
        outs = [jax.ShapeDtypeStruct((rows, width), BF16)]
        outs += [jax.ShapeDtypeStruct((micro + 1,) + shape, BF16) for shape in stored]
        extra = [] if slots is None else list(slots)
        done = kernel_call(
            lambda *refs: forward_kernel(bool(extra), *refs),
            tuple(outs), [SMEM] + [VMEM] * 8 + [ANY] * len(extra), (VMEM, ANY, ANY, ANY),
            scratch=[pltpu.VMEM(shape, BF16) for shape in stored] + [pltpu.SemaphoreType.DMA((2, 3))],
            aliases={9 + at: 1 + at for at in range(len(extra))}, flops=flops, moved=2**24, name="forward",
        )(flag, arrived, ends[min(tick, micro - 1)], qv, qo, sv, so, gains, order, *extra)
        return done[0], done[1:]

    def backward(tick, arrived, slots, sums):
        position = tick - (stages - 1 - z)
        active = (position >= 0) & (position < micro)
        slot = jnp.where(active, position, micro)
        flag = jnp.stack([z == stages - 1, side, slot, active]).astype(I32)
        out, upstream, vgrad = kernel_call(
            backward_kernel,
            (jax.ShapeDtypeStruct((rows, width), BF16), jax.ShapeDtypeStruct((2, rows, width), BF16),
             jax.ShapeDtypeStruct((2, rows, value_width), BF16)),
            [SMEM, VMEM, VMEM, ANY] + [VMEM] * 6, (VMEM,) * 3,
            scratch=[pltpu.VMEM((2, rows, width), BF16), pltpu.SemaphoreType.DMA], flops=flops, moved=2**24, name="backward",
        )(flag, arrived, ends[min(tick, micro - 1)], slots[0], qv, qo, sv, so, gains, unorder)
        sums = kernel_call(
            grads_kernel,
            (jax.ShapeDtypeStruct((2, groups_v, value_width), F32), jax.ShapeDtypeStruct((2, groups_o, width), F32)),
            [SMEM, VMEM, VMEM, ANY, ANY, VMEM, VMEM], (VMEM, VMEM),
            scratch=[pltpu.VMEM(uv_shape, BF16), pltpu.VMEM(uo_shape, BF16), pltpu.SemaphoreType.DMA((2, 2))],
            flops=10**7, moved=2**23, name="grads",
        )(flag, upstream, vgrad, slots[1], slots[2], *sums)
        return out, sums

    ticks = micro + stages - 1
    sums = (jnp.zeros((2, groups_v, value_width), F32), jnp.zeros((2, groups_o, width), F32))
    up_routes = [(source, source + 2) for source in range(section_count - 2)]
    down_routes = [(source + 2, source) for source in range(section_count - 2)]
    arrived_f = arrived_b = jnp.zeros((rows, width), BF16)
    for tick in range(ticks + stages):
        if tick < ticks:
            out, slots = forward(tick, arrived_f, slots)
            if tick < ticks - 1:
                arrived_f = lax.ppermute(out, "section", up_routes)
        if tick >= stages:
            out, sums = backward(tick - stages, arrived_b, slots, sums)
            if tick < ticks + stages - 1:
                arrived_b = lax.ppermute(out, "section", down_routes)

    total_v = sums[0].reshape(2, groups_v, dp_count, -1).transpose(0, 2, 1, 3).reshape(2, dp_count, -1)
    total_o = sums[1].reshape(2, groups_o, dp_count, -1).transpose(0, 2, 1, 3).reshape(2, dp_count, -1)
    total = scatter_sums(jnp.concatenate([total_v, total_o], axis=2), side)
    return total[:count_v].reshape(steps_v.shape), total[count_v:].reshape(steps_o.shape)


def solution(mesh):
    return jax.shard_map(
        on_device,
        mesh=mesh,
        in_specs=(
            P(None, "dp", "section"),
            P(None, "dp", "section"),
            P("section", None, None),
            P("section", None, None),
            P("section", None, "dp"),
            P("section", None, None),
            P("section", None, None),
            P("section", None, "dp"),
            P("section", None),
        ),
        out_specs=(P("section", None, "dp"), P("section", None, "dp")),
        check_vma=False,
    )
```

time: 1670 us -> 607 us (0.36)
  the two profiles are of different devices: /device:TPU:128 before, /device:TPU:232 now
where the time goes in v1:
time: 607 us; the launch traced here: 597 us
  Pallas kernels  182 us (30%)
  waiting for transfers between devices  167 us (28%)
  starting transfers between devices  137 us (23%)
  local copies, waits for them, and re-layouts  96.2 us (16%)
  other arithmetic  11.8 us (2%)
    unnamed x217, local copies, waits for them, and re-layouts  86.7 us
    pallas_call x11, Pallas kernels, backward(): kernel_call(backward_kernel, (jax.ShapeDtypeStruct((rows, width), BF16),...  75.3 us
    ppermute x16, waiting for transfers between devices, fixed_swap(): lax.ppermute(value, axis, [(source, source ^ bit) for source in range(cou...  72.3 us
    pallas_call x11, Pallas kernels, forward(): kernel_call(lambda *refs: forward_kernel(bool(extra), *refs), tuple(outs)...  63.3 us
    ppermute x10, waiting for transfers between devices, on_device(): arrived_b = lax.ppermute(out, 'section', down_routes)  52.7 us
    ppermute x10, starting transfers between devices, on_device(): arrived_f = lax.ppermute(out, 'section', up_routes)  49.6 us
    ppermute x16, starting transfers between devices, fixed_swap(): lax.ppermute(value, axis, [(source, source ^ bit) for source in range(cou...  46.1 us
    ppermute x10, waiting for transfers between devices, on_device(): arrived_f = lax.ppermute(out, 'section', up_routes)  40.1 us
  transfers between devices with their start and end apart: 38, of which 27 were waited for; matrix products, arithmetic and copies ran while one was open for 3% of the time, Pallas kernels for 9%

profile of v1, /device:TPU:232, one launch (start us, length us, event | category | flops | bytes accessed | tf_op | source)
XLA Modules:
  0.0 596.9 jit_solution(16420669844117964181)
XLA Ops:
  29.1 43.6 %collective-permute-done.8 = f32[2,2,2048]{2,1,0:T(2,128)S(1)} collective-permute-done((f32[2,2,2048]{2,1,0:T(2,128)S(1)}, f32[2,2,2048]{2,1,0:T(2,128)S(1)}, u32[]{:S(2)}, u32[]{:S(2)}) %collective-permute-start.8) | collective-permute-done | bytes 32800 | tf_op jit(solution)/shard_map/ppermute | solution.py:284
  93.2 20.2 %collective-permute-start.3 = (bf16[4,16,4096]{2,1,0:T(8,128)(2,1)}, bf16[4,16,4096]{2,1,0:T(8,128)(2,1)}, u32[]{:S(2)}, u32[]{:S(2)}) collective-permute-start(bf16[4,16,4096]{2,1,0:T(8,128)(2,1)} %pad_maximum_fusion), channel_id=1, source_target_pairs={{256,0},{192,448},{288,32},{224,480},{257,1},{193,449},{289,33},{2... | collective-permute-start | bytes 1572872 | tf_op jit(solution)/shard_map/ppermute | solution.py:312
  123.2 13.0 %unpack.1 = (f8e4m3fn[2,8192,512]{2,1,0:T(32,128)(4,1)S(1)}, f8e4m3fn[2,512,8192]{2,1,0:T(32,128)(4,1)S(1)}) custom-call(s32[576,512]{1,0:T(8,128)S(1)} %pad_add_fusion.1.own_v_ref, s32[576,512]{1,0:T(8,128)} %collective-permute-done.4.far_v_ref, s32[36,8192]{1,0:T(8,128)S(1)} %pad_add_fusion.own_o_ref, s32[36,8192]{1,0:T(8,128)} %collective-permute-done.5.far_o_ref), custom_call_target="tpu_custom_call" | custom-call | flops 100000000 | bytes 4194304 | tf_op jit(solution)/shard_map/unpack/pallas_call | solution.py:368
  136.4 6.3 %forward.11 = (bf16[16,8192]{1,0:T(8,128)(2,1)S(1)}, bf16[5,2,16,8192]{3,2,1,0:T(8,128)(2,1)S(1)}, bf16[5,2,64,16,512]{4,3,2,1,0:T(8,128)(2,1)S(1)}, bf16[5,2,4,16,8192]{4,3,2,1,0:T(8,128)(2,1)}) custom-call(s32[3]{0:T(128)S(1)} %copy-done.89, bf16[16,8192]{1,0:T(8,128)(2,1)S(1)} %broadcast_in_dim.17.refs_1_.arrived_ref, ...), custom_call_target="tpu_custom_call" | custom-call | flops 1073741824 | bytes 16777216 | tf_op jit(solution)/shard_map/forward/pallas_call | solution.py:387
  144.6 8.3 %collective-permute-done.12.refs_1_ = bf16[16,8192]{1,0:T(8,128)(2,1)S(1)} collective-permute-done((bf16[16,8192]{1,0:T(8,128)(2,1)S(1)}, bf16[16,8192]{1,0:T(8,128)(2,1)S(1)}, u32[]{:S(2)}, u32[]{:S(2)}) %collective-permute-start.12) | collective-permute-done | bytes 262176 | tf_op jit(solution)/shard_map/ppermute | solution.py:425
  161.9 5.9 collective-permute-done.13.refs_1_
  203.4 5.6 collective-permute-start.16
  233.3 5.6 collective-permute-start.18
  238.9 6.5 %collective-permute-done.18.refs_1_ = bf16[16,8192]{1,0:T(8,128)(2,1)S(1)} collective-permute-done((bf16[16,8192]{1,0:T(8,128)(2,1)S(1)}, bf16[16,8192]{1,0:T(8,128)(2,1)S(1)}, u32[]{:S(2)}, u32[]{:S(2)}) %collective-permute-start.18) | collective-permute-done | bytes 262176 | tf_op jit(solution)/shard_map/ppermute | solution.py:425
  245.5 6.2 %forward.18 = (bf16[16,8192]{1,0:T(8,128)(2,1)}, bf16[5,2,16,8192]{3,2,1,0:T(8,128)(2,1)S(1)}, bf16[5,2,64,16,512]{4,3,2,1,0:T(8,128)(2,1)S(1)}, bf16[5,2,4,16,8192]{4,3,2,1,0:T(8,128)(2,1)}) custom-call(s32[3]{0:T(128)S(1)} %get-tuple-element.244.refs_0_, ...), custom_call_target="tpu_custom_call", output_to_operand_aliasing={{1}: (9, {}), {2}: (10, {}), {3}: (11, {})} | custom-call | flops 1073741824 | bytes 16777216 | tf_op jit(solution)/shard_map/forward/pallas_call | solution.py:387
  283.0 6.2 %forward.19 = (bf16[16,8192]{1,0:T(8,128)(2,1)}, bf16[5,2,16,8192]{3,2,1,0:T(8,128)(2,1)S(1)}, bf16[5,2,64,16,512]{4,3,2,1,0:T(8,128)(2,1)S(1)}, bf16[5,2,4,16,8192]{4,3,2,1,0:T(8,128)(2,1)}) custom-call(s32[3]{0:T(128)S(1)} %get-tuple-element.245.refs_0_, ...), custom_call_target="tpu_custom_call", output_to_operand_aliasing={{1}: (9, {}), {2}: (10, {}), {3}: (11, {})} | custom-call | flops 1073741824 | bytes 16777216 | tf_op jit(solution)/shard_map/forward/pallas_call | solution.py:387
  294.6 5.7 collective-permute-start.21
  306.9 6.6 %backward.11 = (bf16[16,8192]{1,0:T(8,128)(2,1)S(1)}, bf16[2,16,8192]{2,1,0:T(8,128)(2,1)S(1)}, bf16[2,16,512]{2,1,0:T(8,128)(2,1)S(1)}) custom-call(s32[4]{0:T(128)S(1)} %get-tuple-element.210.flag_ref, bf16[16,8192]{1,0:T(8,128)(2,1)S(1)} %copy-done.51, bf16[16,8192]{1,0:T(8,128)(2,1)S(1)} %copy-done.53, bf16[5,2,16,8192]{3,2,1,0:T(8,128)(2,1)S(1)} %copy-done.21, ...), custom_call_target="tpu_custom_call" | custom-call | flops 1073741824 | bytes 16777216 | tf_op jit(solution)/shard_map/backward/pallas_call | solution.py:400
  343.9 6.7 %backward.12 = (bf16[16,8192]{1,0:T(8,128)(2,1)S(1)}, bf16[2,16,8192]{2,1,0:T(8,128)(2,1)S(1)}, bf16[2,16,512]{2,1,0:T(8,128)(2,1)S(1)}) custom-call(s32[4]{0:T(128)S(1)} %get-tuple-element.248.flag_ref, bf16[16,8192]{1,0:T(8,128)(2,1)S(1)} %collective-permute-done.20.arrived_ref, bf16[16,8192]{1,0:T(8,128)(2,1)S(1)} %copy-done.49, ...), custom_call_target="tpu_custom_call" | custom-call | flops 1073741824 | bytes 16777216 | tf_op jit(solution)/shard_map/backward/pallas_call | solution.py:400
  366.6 6.2 %forward.21 = (bf16[16,8192]{1,0:T(8,128)(2,1)}, bf16[5,2,16,8192]{3,2,1,0:T(8,128)(2,1)S(1)}, bf16[5,2,64,16,512]{4,3,2,1,0:T(8,128)(2,1)S(1)}, bf16[5,2,4,16,8192]{4,3,2,1,0:T(8,128)(2,1)}) custom-call(s32[3]{0:T(128)S(1)} %copy-done.86, ...), custom_call_target="tpu_custom_call", output_to_operand_aliasing={{1}: (9, {}), {2}: (10, {}), {3}: (11, {})} | custom-call | flops 1073741824 | bytes 16777216 | tf_op jit(solution)/shard_map/forward/pallas_call | solution.py:387
  372.9 6.7 %backward.13 = (bf16[16,8192]{1,0:T(8,128)(2,1)S(1)}, bf16[2,16,8192]{2,1,0:T(8,128)(2,1)S(1)}, bf16[2,16,512]{2,1,0:T(8,128)(2,1)S(1)}) custom-call(s32[4]{0:T(128)S(1)} %get-tuple-element.249.flag_ref, bf16[16,8192]{1,0:T(8,128)(2,1)S(1)} %collective-permute-done.22.arrived_ref, bf16[16,8192]{1,0:T(8,128)(2,1)S(1)} %copy-done.47, ...), custom_call_target="tpu_custom_call" | custom-call | flops 1073741824 | bytes 16777216 | tf_op jit(solution)/shard_map/backward/pallas_call | solution.py:400
  382.9 7.5 %collective-permute-done.24.arrived_ref = bf16[16,8192]{1,0:T(8,128)(2,1)S(1)} collective-permute-done((bf16[16,8192]{1,0:T(8,128)(2,1)S(1)}, bf16[16,8192]{1,0:T(8,128)(2,1)S(1)}, u32[]{:S(2)}, u32[]{:S(2)}) %collective-permute-start.24) | collective-permute-done | bytes 262176 | tf_op jit(solution)/shard_map/ppermute | solution.py:429
  390.5 6.7 %backward.14 = (bf16[16,8192]{1,0:T(8,128)(2,1)S(1)}, bf16[2,16,8192]{2,1,0:T(8,128)(2,1)S(1)}, bf16[2,16,512]{2,1,0:T(8,128)(2,1)S(1)}) custom-call(s32[4]{0:T(128)S(1)} %get-tuple-element.250.flag_ref, bf16[16,8192]{1,0:T(8,128)(2,1)S(1)} %collective-permute-done.24.arrived_ref, bf16[16,8192]{1,0:T(8,128)(2,1)S(1)} %copy-done.38, ...), custom_call_target="tpu_custom_call" | custom-call | flops 1073741824 | bytes 16777216 | tf_op jit(solution)/shard_map/backward/pallas_call | solution.py:400
  399.1 7.5 %collective-permute-done.25.arrived_ref = bf16[16,8192]{1,0:T(8,128)(2,1)S(1)} collective-permute-done((bf16[16,8192]{1,0:T(8,128)(2,1)S(1)}, bf16[16,8192]{1,0:T(8,128)(2,1)S(1)}, u32[]{:S(2)}, u32[]{:S(2)}) %collective-permute-start.25) | collective-permute-done | bytes 262176 | tf_op jit(solution)/shard_map/ppermute | solution.py:429
  406.6 6.7 %backward.15 = (bf16[16,8192]{1,0:T(8,128)(2,1)S(1)}, bf16[2,16,8192]{2,1,0:T(8,128)(2,1)S(1)}, bf16[2,16,512]{2,1,0:T(8,128)(2,1)S(1)}) custom-call(s32[4]{0:T(128)S(1)} %get-tuple-element.251.flag_ref, bf16[16,8192]{1,0:T(8,128)(2,1)S(1)} %collective-permute-done.25.arrived_ref, bf16[16,8192]{1,0:T(8,128)(2,1)S(1)} %copy-done.38, ...), custom_call_target="tpu_custom_call" | custom-call | flops 1073741824 | bytes 16777216 | tf_op jit(solution)/shard_map/backward/pallas_call | solution.py:400
  415.4 7.4 %collective-permute-done.26.arrived_ref = bf16[16,8192]{1,0:T(8,128)(2,1)S(1)} collective-permute-done((bf16[16,8192]{1,0:T(8,128)(2,1)S(1)}, bf16[16,8192]{1,0:T(8,128)(2,1)S(1)}, u32[]{:S(2)}, u32[]{:S(2)}) %collective-permute-start.26) | collective-permute-done | bytes 262176 | tf_op jit(solution)/shard_map/ppermute | solution.py:429
  422.8 6.7 %backward.16 = (bf16[16,8192]{1,0:T(8,128)(2,1)S(1)}, bf16[2,16,8192]{2,1,0:T(8,128)(2,1)S(1)}, bf16[2,16,512]{2,1,0:T(8,128)(2,1)S(1)}) custom-call(s32[4]{0:T(128)S(1)} %get-tuple-element.252.flag_ref, bf16[16,8192]{1,0:T(8,128)(2,1)S(1)} %collective-permute-done.26.arrived_ref, bf16[16,8192]{1,0:T(8,128)(2,1)S(1)} %copy-done.38, ...), custom_call_target="tpu_custom_call" | custom-call | flops 1073741824 | bytes 16777216 | tf_op jit(solution)/shard_map/backward/pallas_call | solution.py:400
  431.5 7.5 %collective-permute-done.27.arrived_ref = bf16[16,8192]{1,0:T(8,128)(2,1)S(1)} collective-permute-done((bf16[16,8192]{1,0:T(8,128)(2,1)S(1)}, bf16[16,8192]{1,0:T(8,128)(2,1)S(1)}, u32[]{:S(2)}, u32[]{:S(2)}) %collective-permute-start.27) | collective-permute-done | bytes 262176 | tf_op jit(solution)/shard_map/ppermute | solution.py:429
  439.0 6.7 %backward.17 = (bf16[16,8192]{1,0:T(8,128)(2,1)S(1)}, bf16[2,16,8192]{2,1,0:T(8,128)(2,1)S(1)}, bf16[2,16,512]{2,1,0:T(8,128)(2,1)S(1)}) custom-call(s32[4]{0:T(128)S(1)} %get-tuple-element.253.flag_ref, bf16[16,8192]{1,0:T(8,128)(2,1)S(1)} %collective-permute-done.27.arrived_ref, bf16[16,8192]{1,0:T(8,128)(2,1)S(1)} %copy-done.38, ...), custom_call_target="tpu_custom_call" | custom-call | flops 1073741824 | bytes 16777216 | tf_op jit(solution)/shard_map/backward/pallas_call | solution.py:400
  447.6 7.5 %collective-permute-done.28.arrived_ref = bf16[16,8192]{1,0:T(8,128)(2,1)S(1)} collective-permute-done((bf16[16,8192]{1,0:T(8,128)(2,1)S(1)}, bf16[16,8192]{1,0:T(8,128)(2,1)S(1)}, u32[]{:S(2)}, u32[]{:S(2)}) %collective-permute-start.28) | collective-permute-done | bytes 262176 | tf_op jit(solution)/shard_map/ppermute | solution.py:429
  455.2 6.7 %backward.18 = (bf16[16,8192]{1,0:T(8,128)(2,1)S(1)}, bf16[2,16,8192]{2,1,0:T(8,128)(2,1)S(1)}, bf16[2,16,512]{2,1,0:T(8,128)(2,1)S(1)}) custom-call(s32[4]{0:T(128)S(1)} %get-tuple-element.254.flag_ref, bf16[16,8192]{1,0:T(8,128)(2,1)S(1)} %collective-permute-done.28.arrived_ref, bf16[16,8192]{1,0:T(8,128)(2,1)S(1)} %copy-done.38, ...), custom_call_target="tpu_custom_call" | custom-call | flops 1073741824 | bytes 16777216 | tf_op jit(solution)/shard_map/backward/pallas_call | solution.py:400
  463.8 7.5 %collective-permute-done.29.arrived_ref = bf16[16,8192]{1,0:T(8,128)(2,1)S(1)} collective-permute-done((bf16[16,8192]{1,0:T(8,128)(2,1)S(1)}, bf16[16,8192]{1,0:T(8,128)(2,1)S(1)}, u32[]{:S(2)}, u32[]{:S(2)}) %collective-permute-start.29) | collective-permute-done | bytes 262176 | tf_op jit(solution)/shard_map/ppermute | solution.py:429
  471.4 6.7 %backward.19 = (bf16[16,8192]{1,0:T(8,128)(2,1)S(1)}, bf16[2,16,8192]{2,1,0:T(8,128)(2,1)S(1)}, bf16[2,16,512]{2,1,0:T(8,128)(2,1)S(1)}) custom-call(s32[4]{0:T(128)S(1)} %get-tuple-element.255.flag_ref, bf16[16,8192]{1,0:T(8,128)(2,1)S(1)} %collective-permute-done.29.arrived_ref, bf16[16,8192]{1,0:T(8,128)(2,1)S(1)} %copy-done.38, ...), custom_call_target="tpu_custom_call" | custom-call | flops 1073741824 | bytes 16777216 | tf_op jit(solution)/shard_map/backward/pallas_call | solution.py:400
  481.4 7.5 %collective-permute-done.30.arrived_ref = bf16[16,8192]{1,0:T(8,128)(2,1)S(1)} collective-permute-done((bf16[16,8192]{1,0:T(8,128)(2,1)S(1)}, bf16[16,8192]{1,0:T(8,128)(2,1)S(1)}, u32[]{:S(2)}, u32[]{:S(2)}) %collective-permute-start.30) | collective-permute-done | bytes 262176 | tf_op jit(solution)/shard_map/ppermute | solution.py:429
  489.0 7.4 %backward.20 = (bf16[16,8192]{1,0:T(8,128)(2,1)}, bf16[2,16,8192]{2,1,0:T(8,128)(2,1)S(1)}, bf16[2,16,512]{2,1,0:T(8,128)(2,1)S(1)}) custom-call(s32[4]{0:T(128)S(1)} %get-tuple-element.256.flag_ref, bf16[16,8192]{1,0:T(8,128)(2,1)S(1)} %collective-permute-done.30.arrived_ref, bf16[16,8192]{1,0:T(8,128)(2,1)S(1)} %copy-done.38, ...), custom_call_target="tpu_custom_call" | custom-call | flops 1073741824 | bytes 16777216 | tf_op jit(solution)/shard_map/backward/pallas_call | solution.py:400
  539.1 7.9 %backward.21 = (bf16[16,8192]{1,0:T(8,128)(2,1)}, bf16[2,16,8192]{2,1,0:T(8,128)(2,1)S(1)}, bf16[2,16,512]{2,1,0:T(8,128)(2,1)S(1)}) custom-call(s32[4]{0:T(128)S(1)} %pad_add_fusion.2.flag_ref, bf16[16,8192]{1,0:T(8,128)(2,1)} %collective-permute-done.31.arrived_ref, bf16[16,8192]{1,0:T(8,128)(2,1)S(1)} %copy-done.39, ...), custom_call_target="tpu_custom_call" | custom-call | flops 1073741824 | bytes 16777216 | tf_op jit(solution)/shard_map/backward/pallas_call | solution.py:400
  587.6 7.5 %collective-permute-done.37 = bf16[1,2048]{1,0:T(2,128)(2,1)S(1)} collective-permute-done((bf16[1,2048]{1,0:T(2,128)(2,1)S(1)}, bf16[1,2048]{1,0:T(2,128)(2,1)S(1)}, u32[]{:S(2)}, u32[]{:S(2)}) %collective-permute-start.37) | collective-permute-done | bytes 4128 | tf_op jit(solution)/shard_map/ppermute | solution.py:284
  (368 shorter events, 318.8 us)
Async XLA Ops:
  3.0 19.4 %collective-permute-start.6 = (f32[10240]{0:T(1024)S(1)}, f32[10240]{0:T(1024)S(1)}, u32[]{:S(2)}, u32[]{:S(2)}) collective-permute-start(f32[10240]{0:T(1024)S(1)} %pad_maximum_fusion.11), channel_id=1, source_target_pairs={{0,32},{32,0},{64,96},{96,64},{128,160},{160,128},{192,224},{224,1... | collective-permute-start | bytes 122888 | tf_op jit(solution)/shard_map/ppermute | solution.py:284
  8.9 67.1 %collective-permute-start = (bf16[2,4,16,512]{3,2,1,0:T(8,128)(2,1)S(1)}, bf16[2,4,16,512]{3,2,1,0:T(8,128)(2,1)S(1)}, u32[]{:S(2)}, u32[]{:S(2)}) collective-permute-start(bf16[2,4,16,512]{3,2,1,0:T(8,128)(2,1)S(1)} %broadcast_select_fusion.12), channel_id=1, source_target_pairs={{0,32},{32,0},{64,96},{96,64},{128,160},{160,128},{192,224},{224,1... | collective-permute-start | bytes 393224 | tf_op jit(solution)/shard_map/ppermute | solution.py:284
  13.2 109.9 %collective-permute-start.5 = (s32[36,8192]{1,0:T(8,128)S(1)}, s32[36,8192]{1,0:T(8,128)}, u32[]{:S(2)}, u32[]{:S(2)}) collective-permute-start(s32[36,8192]{1,0:T(8,128)S(1)} %pad_add_fusion.own_o_ref), channel_id=1, source_target_pairs={{0,32},{32,0},{64,96},{96,64},{128,160},{160,128},{192,224},{224,1... | collective-permute-start | bytes 3538952 | tf_op jit(solution)/shard_map/ppermute | solution.py:284
  18.6 104.6 %collective-permute-start.4 = (s32[576,512]{1,0:T(8,128)S(1)}, s32[576,512]{1,0:T(8,128)}, u32[]{:S(2)}, u32[]{:S(2)}) collective-permute-start(s32[576,512]{1,0:T(8,128)S(1)} %pad_add_fusion.1.own_v_ref), channel_id=1, source_target_pairs={{0,32},{32,0},{64,96},{96,64},{128,160},{160,128},{192,224},{224,1... | collective-permute-start | bytes 3538952 | tf_op jit(solution)/shard_map/ppermute | solution.py:284
  25.5 47.1 %collective-permute-start.8 = (f32[2,2,2048]{2,1,0:T(2,128)S(1)}, f32[2,2,2048]{2,1,0:T(2,128)S(1)}, u32[]{:S(2)}, u32[]{:S(2)}) collective-permute-start(f32[2,2,2048]{2,1,0:T(2,128)S(1)} %pad_maximum_fusion.12), channel_id=1, source_target_pairs={{0,2},{1,3},{2,0},{3,1},{4,6},{5,7},{6,4},{7,5},{8,10},{9,11},{10,... | collective-permute-start | bytes 98312 | tf_op jit(solution)/shard_map/ppermute | solution.py:284
  76.1 6.9 %collective-permute-start.1 = (bf16[4,16,1024]{2,1,0:T(8,128)(2,1)S(1)}, bf16[4,16,1024]{2,1,0:T(8,128)(2,1)S(1)}, u32[]{:S(2)}, u32[]{:S(2)}) collective-permute-start(bf16[4,16,1024]{2,1,0:T(8,128)(2,1)S(1)} %select_bitcast_fusion), channel_id=1, source_target_pairs={{0,64},{32,96},{64,0},{96,32},{128,192},{160,224},{192,128},{224,1... | collective-permute-start | bytes 393224 | tf_op jit(solution)/shard_map/ppermute | solution.py:284
  79.0 7.9 %collective-permute-start.10 = (f32[8,2,2048]{2,1,0:T(2,128)S(1)}, f32[8,2,2048]{2,1,0:T(2,128)S(1)}, u32[]{:S(2)}, u32[]{:S(2)}) collective-permute-start(f32[8,2,2048]{2,1,0:T(2,128)S(1)} %pad_maximum_fusion.8), channel_id=1, source_target_pairs={{0,8},{1,9},{2,10},{3,11},{4,12},{5,13},{6,14},{7,15},{8,0},{9,1},... | collective-permute-start | bytes 393224 | tf_op jit(solution)/shard_map/ppermute | solution.py:284
  83.1 9.2 %collective-permute-start.2 = (bf16[4,16,2048]{2,1,0:T(8,128)(2,1)S(1)}, bf16[4,16,2048]{2,1,0:T(8,128)(2,1)S(1)}, u32[]{:S(2)}, u32[]{:S(2)}) collective-permute-start(bf16[4,16,2048]{2,1,0:T(8,128)(2,1)S(1)} %pad_maximum_fusion.4), channel_id=1, source_target_pairs={{128,0},{64,192},{160,32},{96,224},{384,256},{320,448},{416,288},{... | collective-permute-start | bytes 786440 | tf_op jit(solution)/shard_map/ppermute | solution.py:312
  87.2 26.3 %collective-permute-start.11 = (f32[16,2,2048]{2,1,0:T(2,128)S(1)}, f32[16,2,2048]{2,1,0:T(2,128)S(1)}, u32[]{:S(2)}, u32[]{:S(2)}) collective-permute-start(f32[16,2,2048]{2,1,0:T(2,128)S(1)} %pad_maximum_fusion.5), channel_id=1, source_target_pairs={{0,16},{1,17},{2,18},{3,19},{4,20},{5,21},{6,22},{7,23},{8,24},{9,... | collective-permute-start | bytes 786440 | tf_op jit(solution)/shard_map/ppermute | solution.py:284
  93.2 28.5 %collective-permute-start.3 = (bf16[4,16,4096]{2,1,0:T(8,128)(2,1)}, bf16[4,16,4096]{2,1,0:T(8,128)(2,1)}, u32[]{:S(2)}, u32[]{:S(2)}) collective-permute-start(bf16[4,16,4096]{2,1,0:T(8,128)(2,1)} %pad_maximum_fusion), channel_id=1, source_target_pairs={{256,0},{192,448},{288,32},{224,480},{257,1},{193,449},{289,33},{2... | collective-permute-start | bytes 1572872 | tf_op jit(solution)/shard_map/ppermute | solution.py:312
  142.7 10.2 %collective-permute-start.12 = (bf16[16,8192]{1,0:T(8,128)(2,1)S(1)}, bf16[16,8192]{1,0:T(8,128)(2,1)S(1)}, u32[]{:S(2)}, u32[]{:S(2)}) collective-permute-start(bf16[16,8192]{1,0:T(8,128)(2,1)S(1)} %get-tuple-element.103), channel_id=1, source_target_pairs={{0,64},{32,96},{64,128},{96,160},{128,192},{160,224},{192,256},{22... | collective-permute-start | bytes 786440 | tf_op jit(solution)/shard_map/ppermute | solution.py:425
  158.4 9.4 %collective-permute-start.13 = (bf16[16,8192]{1,0:T(8,128)(2,1)S(1)}, bf16[16,8192]{1,0:T(8,128)(2,1)S(1)}, u32[]{:S(2)}, u32[]{:S(2)}) collective-permute-start(bf16[16,8192]{1,0:T(8,128)(2,1)S(1)} %get-tuple-element.107), channel_id=1, source_target_pairs={{0,64},{32,96},{64,128},{96,160},{128,192},{160,224},{192,256},{22... | collective-permute-start | bytes 786440 | tf_op jit(solution)/shard_map/ppermute | solution.py:425
  173.3 9.7 %collective-permute-start.14 = (bf16[16,8192]{1,0:T(8,128)(2,1)S(1)}, bf16[16,8192]{1,0:T(8,128)(2,1)S(1)}, u32[]{:S(2)}, u32[]{:S(2)}) collective-permute-start(bf16[16,8192]{1,0:T(8,128)(2,1)S(1)} %get-tuple-element.111), channel_id=1, source_target_pairs={{0,64},{32,96},{64,128},{96,160},{128,192},{160,224},{192,256},{22... | collective-permute-start | bytes 786440 | tf_op jit(solution)/shard_map/ppermute | solution.py:425
  188.5 9.5 %collective-permute-start.15 = (bf16[16,8192]{1,0:T(8,128)(2,1)S(1)}, bf16[16,8192]{1,0:T(8,128)(2,1)S(1)}, u32[]{:S(2)}, u32[]{:S(2)}) collective-permute-start(bf16[16,8192]{1,0:T(8,128)(2,1)S(1)} %get-tuple-element.115), channel_id=1, source_target_pairs={{0,64},{32,96},{64,128},{96,160},{128,192},{160,224},{192,256},{22... | collective-permute-start | bytes 786440 | tf_op jit(solution)/shard_map/ppermute | solution.py:425
  203.4 9.5 %collective-permute-start.16 = (bf16[16,8192]{1,0:T(8,128)(2,1)S(1)}, bf16[16,8192]{1,0:T(8,128)(2,1)S(1)}, u32[]{:S(2)}, u32[]{:S(2)}) collective-permute-start(bf16[16,8192]{1,0:T(8,128)(2,1)S(1)} %get-tuple-element.119), channel_id=1, source_target_pairs={{0,64},{32,96},{64,128},{96,160},{128,192},{160,224},{192,256},{22... | collective-permute-start | bytes 786440 | tf_op jit(solution)/shard_map/ppermute | solution.py:425
  218.4 9.4 %collective-permute-start.17 = (bf16[16,8192]{1,0:T(8,128)(2,1)S(1)}, bf16[16,8192]{1,0:T(8,128)(2,1)S(1)}, u32[]{:S(2)}, u32[]{:S(2)}) collective-permute-start(bf16[16,8192]{1,0:T(8,128)(2,1)S(1)} %get-tuple-element.123), channel_id=1, source_target_pairs={{0,64},{32,96},{64,128},{96,160},{128,192},{160,224},{192,256},{22... | collective-permute-start | bytes 786440 | tf_op jit(solution)/shard_map/ppermute | solution.py:425
  233.3 12.1 %collective-permute-start.18 = (bf16[16,8192]{1,0:T(8,128)(2,1)S(1)}, bf16[16,8192]{1,0:T(8,128)(2,1)S(1)}, u32[]{:S(2)}, u32[]{:S(2)}) collective-permute-start(bf16[16,8192]{1,0:T(8,128)(2,1)S(1)} %get-tuple-element.127), channel_id=1, source_target_pairs={{0,64},{32,96},{64,128},{96,160},{128,192},{160,224},{192,256},{22... | collective-permute-start | bytes 786440 | tf_op jit(solution)/shard_map/ppermute | solution.py:425
  257.1 9.8 %collective-permute-start.19 = (bf16[16,8192]{1,0:T(8,128)(2,1)}, bf16[16,8192]{1,0:T(8,128)(2,1)S(1)}, u32[]{:S(2)}, u32[]{:S(2)}) collective-permute-start(bf16[16,8192]{1,0:T(8,128)(2,1)} %get-tuple-element.131), channel_id=1, source_target_pairs={{0,64},{32,96},{64,128},{96,160},{128,192},{160,224},{192,256},{22... | collective-permute-start | bytes 786440 | tf_op jit(solution)/shard_map/ppermute | solution.py:425
  294.6 28.5 %collective-permute-start.21 = (bf16[16,8192]{1,0:T(8,128)(2,1)}, bf16[16,8192]{1,0:T(8,128)(2,1)S(1)}, u32[]{:S(2)}, u32[]{:S(2)}) collective-permute-start(bf16[16,8192]{1,0:T(8,128)(2,1)} %get-tuple-element.137), channel_id=1, source_target_pairs={{0,64},{32,96},{64,128},{96,160},{128,192},{160,224},{192,256},{22... | collective-permute-start | bytes 786440 | tf_op jit(solution)/shard_map/ppermute | solution.py:425
  313.6 28.5 %collective-permute-start.20 = (bf16[16,8192]{1,0:T(8,128)(2,1)S(1)}, bf16[16,8192]{1,0:T(8,128)(2,1)S(1)}, u32[]{:S(2)}, u32[]{:S(2)}) collective-permute-start(bf16[16,8192]{1,0:T(8,128)(2,1)S(1)} %get-tuple-element.136), channel_id=1, source_target_pairs={{64,0},{96,32},{128,64},{160,96},{192,128},{224,160},{256,192},{28... | collective-permute-start | bytes 786440 | tf_op jit(solution)/shard_map/ppermute | solution.py:429
  337.0 22.7 %collective-permute-start.23 = (bf16[16,8192]{1,0:T(8,128)(2,1)S(1)}, bf16[16,8192]{1,0:T(8,128)(2,1)S(1)}, u32[]{:S(2)}, u32[]{:S(2)}) collective-permute-start(bf16[16,8192]{1,0:T(8,128)(2,1)S(1)} %get-tuple-element.142), channel_id=1, source_target_pairs={{0,64},{32,96},{64,128},{96,160},{128,192},{160,224},{192,256},{22... | collective-permute-start | bytes 786440 | tf_op jit(solution)/shard_map/ppermute | solution.py:425
  350.6 22.3 %collective-permute-start.22 = (bf16[16,8192]{1,0:T(8,128)(2,1)S(1)}, bf16[16,8192]{1,0:T(8,128)(2,1)S(1)}, u32[]{:S(2)}, u32[]{:S(2)}) collective-permute-start(bf16[16,8192]{1,0:T(8,128)(2,1)S(1)} %get-tuple-element.141), channel_id=1, source_target_pairs={{64,0},{96,32},{128,64},{160,96},{192,128},{224,160},{256,192},{28... | collective-permute-start | bytes 786440 | tf_op jit(solution)/shard_map/ppermute | solution.py:429
  381.0 9.5 %collective-permute-start.24 = (bf16[16,8192]{1,0:T(8,128)(2,1)S(1)}, bf16[16,8192]{1,0:T(8,128)(2,1)S(1)}, u32[]{:S(2)}, u32[]{:S(2)}) collective-permute-start(bf16[16,8192]{1,0:T(8,128)(2,1)S(1)} %get-tuple-element.146), channel_id=1, source_target_pairs={{64,0},{96,32},{128,64},{160,96},{192,128},{224,160},{256,192},{28... | collective-permute-start | bytes 786440 | tf_op jit(solution)/shard_map/ppermute | solution.py:429
  397.2 9.5 %collective-permute-start.25 = (bf16[16,8192]{1,0:T(8,128)(2,1)S(1)}, bf16[16,8192]{1,0:T(8,128)(2,1)S(1)}, u32[]{:S(2)}, u32[]{:S(2)}) collective-permute-start(bf16[16,8192]{1,0:T(8,128)(2,1)S(1)} %get-tuple-element.147), channel_id=1, source_target_pairs={{64,0},{96,32},{128,64},{160,96},{192,128},{224,160},{256,192},{28... | collective-permute-start | bytes 786440 | tf_op jit(solution)/shard_map/ppermute | solution.py:429
  413.3 9.5 %collective-permute-start.26 = (bf16[16,8192]{1,0:T(8,128)(2,1)S(1)}, bf16[16,8192]{1,0:T(8,128)(2,1)S(1)}, u32[]{:S(2)}, u32[]{:S(2)}) collective-permute-start(bf16[16,8192]{1,0:T(8,128)(2,1)S(1)} %get-tuple-element.148), channel_id=1, source_target_pairs={{64,0},{96,32},{128,64},{160,96},{192,128},{224,160},{256,192},{28... | collective-permute-start | bytes 786440 | tf_op jit(solution)/shard_map/ppermute | solution.py:429
  429.5 9.5 %collective-permute-start.27 = (bf16[16,8192]{1,0:T(8,128)(2,1)S(1)}, bf16[16,8192]{1,0:T(8,128)(2,1)S(1)}, u32[]{:S(2)}, u32[]{:S(2)}) collective-permute-start(bf16[16,8192]{1,0:T(8,128)(2,1)S(1)} %get-tuple-element.149), channel_id=1, source_target_pairs={{64,0},{96,32},{128,64},{160,96},{192,128},{224,160},{256,192},{28... | collective-permute-start | bytes 786440 | tf_op jit(solution)/shard_map/ppermute | solution.py:429
  445.7 9.5 %collective-permute-start.28 = (bf16[16,8192]{1,0:T(8,128)(2,1)S(1)}, bf16[16,8192]{1,0:T(8,128)(2,1)S(1)}, u32[]{:S(2)}, u32[]{:S(2)}) collective-permute-start(bf16[16,8192]{1,0:T(8,128)(2,1)S(1)} %get-tuple-element.150), channel_id=1, source_target_pairs={{64,0},{96,32},{128,64},{160,96},{192,128},{224,160},{256,192},{28... | collective-permute-start | bytes 786440 | tf_op jit(solution)/shard_map/ppermute | solution.py:429
  461.9 9.5 %collective-permute-start.29 = (bf16[16,8192]{1,0:T(8,128)(2,1)S(1)}, bf16[16,8192]{1,0:T(8,128)(2,1)S(1)}, u32[]{:S(2)}, u32[]{:S(2)}) collective-permute-start(bf16[16,8192]{1,0:T(8,128)(2,1)S(1)} %get-tuple-element.151), channel_id=1, source_target_pairs={{64,0},{96,32},{128,64},{160,96},{192,128},{224,160},{256,192},{28... | collective-permute-start | bytes 786440 | tf_op jit(solution)/shard_map/ppermute | solution.py:429
  479.5 9.5 %collective-permute-start.30 = (bf16[16,8192]{1,0:T(8,128)(2,1)S(1)}, bf16[16,8192]{1,0:T(8,128)(2,1)S(1)}, u32[]{:S(2)}, u32[]{:S(2)}) collective-permute-start(bf16[16,8192]{1,0:T(8,128)(2,1)S(1)} %get-tuple-element.152), channel_id=1, source_target_pairs={{64,0},{96,32},{128,64},{160,96},{192,128},{224,160},{256,192},{28... | collective-permute-start | bytes 786440 | tf_op jit(solution)/shard_map/ppermute | solution.py:429
  497.8 33.9 %collective-permute-start.31 = (bf16[16,8192]{1,0:T(8,128)(2,1)}, bf16[16,8192]{1,0:T(8,128)(2,1)}, u32[]{:S(2)}, u32[]{:S(2)}) collective-permute-start(bf16[16,8192]{1,0:T(8,128)(2,1)} %get-tuple-element.153), channel_id=1, source_target_pairs={{64,0},{96,32},{128,64},{160,96},{192,128},{224,160},{256,192},{28... | collective-permute-start | bytes 786440 | tf_op jit(solution)/shard_map/ppermute | solution.py:429
  555.2 8.4 %collective-permute-start.32 = (bf16[32,2048]{1,0:T(8,128)(2,1)S(1)}, bf16[32,2048]{1,0:T(8,128)(2,1)S(1)}, u32[]{:S(2)}, u32[]{:S(2)}) collective-permute-start(bf16[32,2048]{1,0:T(8,128)(2,1)S(1)} %fusion.16), channel_id=1, source_target_pairs={{0,32},{32,0},{64,96},{96,64},{128,160},{160,128},{192,224},{224,1... | collective-permute-start | bytes 393224 | tf_op jit(solution)/shard_map/ppermute | solution.py:284
  585.6 9.5 %collective-permute-start.37 = (bf16[1,2048]{1,0:T(2,128)(2,1)S(1)}, bf16[1,2048]{1,0:T(2,128)(2,1)S(1)}, u32[]{:S(2)}, u32[]{:S(2)}) collective-permute-start(bf16[1,2048]{1,0:T(2,128)(2,1)S(1)} %fusion.28), channel_id=1, source_target_pairs={{0,16},{1,17},{2,18},{3,19},{4,20},{5,21},{6,22},{7,23},{8,24},{9,... | collective-permute-start | bytes 12296 | tf_op jit(solution)/shard_map/ppermute | solution.py:284
  (111 other events, 1449.4 us)
